TPU v7x, 32 devices: a whole 2x2x4 slice. The times are simulated.
32 devices in a mesh: group: 2 (over x), brick: 16 (over z, y, core).
Axes of the slice: x: 2, y: 2, z: 4, core: 2. Of those that a mesh axis runs over, the one named last changes fastest.
Arguments:
- subjects: float32 [4, 128, 64, 256], P('group', 'brick'), parts along dimension 0, may hold values from -24 to 24
- template: float32 [256, 64, 256], P(('group', 'brick')), parts along dimension 0, may hold values from -8 to 8
Outputs:
- atlas: float32 [256, 64, 256], P(('group', 'brick')), parts along dimension 0
- fields: float32 [3, 4, 128, 64, 256], P(None, 'group', 'brick'), parts along dimension 1
There are 2 independent parts, one for each index of `group`. A program takes and returns all parts, laid end to end along the dimension named above; each array names one. Nothing has to cross between parts.
All inputs are finite; a program needn't handle non-finite values.
Results may differ from a plain program's by a relative error of at most 0.0001.
Values sent between devices are 32-bit elements; how exact they have to be, the bound alone decides.
A program may use at most 64 MiB of HBM per device.

v0:
```python
import math

import jax
import jax.numpy as jnp
from jax import lax
from jax.sharding import PartitionSpec as P

RAD = 2
ROUNDS = 2
ITERS = 3


SIGMA = 1.5
STEP = 1.0
KAPPA = 0.5
EPS = 1e-05


def padded_2(shard, sides, width):
    for axis, dim in sides:
        count, length = (lax.axis_size(axis), shard.shape[dim])
        up = [(i, (i + 1) % count) for i in range(count - 1)]
        down = [(j, i) for i, j in up]
        last = lax.slice_in_dim(shard, length - width, length, axis=dim)
        initial = lax.slice_in_dim(shard, 0, width, axis=dim)
        before = lax.ppermute(last, axis, up)
        after = lax.ppermute(initial, axis, down)
        shard = jnp.concatenate([before, shard, after], axis=dim)
    return shard


def taps_list(radius):
    raw = [math.exp(-(k * k) / (2.0 * SIGMA * SIGMA)) for k in range(-radius, radius + 1)]
    total = 0.0
    for value in raw:
        total = total + value
    return [value / total for value in raw]


def hat(value):
    return jnp.maximum(0.0, 1.0 - jnp.abs(value))


def pad_last(volume):
    return jnp.pad(volume, [(0, 0)] * (volume.ndim - 2) + [(1, 1), (1, 1)])


def warp_image(padded, disp):
    planes, rows, cols = (disp.shape[2], disp.shape[3], disp.shape[4])
    first_w = [hat(disp[0] - a) for a in (-1, 0, 1)]
    second_w = [hat(disp[1] - b) for b in (-1, 0, 1)]
    third_w = [hat(disp[2] - c) for c in (-1, 0, 1)]
    result = jnp.zeros(disp.shape[1:], jnp.float32)
    for ia, a in enumerate((-1, 0, 1)):
        inner = jnp.zeros(disp.shape[1:], jnp.float32)
        for ib, b in enumerate((-1, 0, 1)):
            line = jnp.zeros(disp.shape[1:], jnp.float32)
            for ic, c in enumerate((-1, 0, 1)):
                piece = padded[
                    :, 1 + a : 1 + a + planes, 1 + b : 1 + b + rows, 1 + c : 1 + c + cols
                ]
                line = line + third_w[ic] * piece
            inner = inner + second_w[ib] * line
        result = result + first_w[ia] * inner
    return result


def gradient(tpad):
    g_first = (tpad[2:, 1:-1, 1:-1] - tpad[:-2, 1:-1, 1:-1]) * 0.5
    g_second = (tpad[1:-1, 2:, 1:-1] - tpad[1:-1, :-2, 1:-1]) * 0.5
    g_third = (tpad[1:-1, 1:-1, 2:] - tpad[1:-1, 1:-1, :-2]) * 0.5
    return jnp.stack([g_first, g_second, g_third])


def forces(state, warped, current, grads):
    diff = current[None] - warped
    denom = (
        (grads[0] * grads[0] + grads[1] * grads[1] + grads[2] * grads[2])[None]
        + diff * diff
        + KAPPA
    )
    ratio = STEP * diff / denom
    return state + grads[:, None] * ratio[None]


def first_pass(extended, planes):
    taps = taps_list(RAD)
    result = taps[0] * lax.slice_in_dim(extended, 0, planes, axis=2)
    for k in range(1, 2 * RAD + 1):
        result = result + taps[k] * lax.slice_in_dim(extended, k, k + planes, axis=2)
    return result


def along_axis(volume, axis):
    taps = taps_list(RAD)
    size_here = volume.shape[axis]
    pads = [(0, 0)] * volume.ndim
    pads[axis] = (RAD, RAD)
    padded = jnp.pad(volume, pads)
    result = taps[0] * lax.slice_in_dim(padded, 0, size_here, axis=axis)
    for k in range(1, 2 * RAD + 1):
        result = result + taps[k] * lax.slice_in_dim(padded, k, k + size_here, axis=axis)
    return result


def normalize(mean_image, count):
    mu = lax.psum(jnp.sum(mean_image), "brick") / count
    centered = mean_image - mu
    var = lax.psum(jnp.sum(centered * centered), "brick") / count
    return centered / jnp.sqrt(var + EPS)


def per_device(subjects, template):
    planes = subjects.shape[1]
    total_planes = planes * lax.axis_size("brick")
    count = total_planes * subjects.shape[2] * subjects.shape[3]
    fields = jnp.zeros((3,) + subjects.shape, jnp.float32)
    current = template
    image_pad = pad_last(padded_2(subjects, (("brick", 1),), 1))
    for rnd in range(ROUNDS):
        tpad = pad_last(padded_2(current, (("brick", 0),), 1))
        grads = gradient(tpad)
        for step in range(ITERS):
            warped = warp_image(image_pad, jnp.tanh(fields))
            update = forces(fields, warped, current, grads)
            wide = padded_2(update, (("brick", 2),), RAD)
            fields = along_axis(along_axis(first_pass(wide, planes), 3), 4)
        warped = warp_image(image_pad, jnp.tanh(fields))
        current = normalize(jnp.mean(warped, axis=0), count)
    return (current, fields)


def solution(mesh):
    return jax.shard_map(
        per_device,
        mesh=mesh,
        in_specs=(P("group", "brick", None, None), P(("group", "brick"), None, None)),
        out_specs=(P(("group", "brick"), None, None), P(None, "group", "brick", None, None)),
        check_vma=False,
    )
```

profile of v0, /device:TPU:0, one launch (start us, length us, event | category | flops | bytes accessed | tf_op | source)
XLA Modules:
  0.0 384.3 jit_solution(855583789614790249)
XLA Ops:
  6.9 4.5 %collective-permute-start.2 = (f32[2,1,64,256]{3,2,1,0:T(8,128)S(1)}, f32[2,1,64,256]{3,2,1,0:T(8,128)S(1)}, u32[]{:S(2)}, u32[]{:S(2)}) collective-permute-start(f32[2,1,64,256]{3,2,1,0:T(8,128)S(1)} %get-tuple-element.34), channel_id=1, source_target_pairs={{0,1},{1,2},{2,3},{3,4},{4,5},{5,6},{6,7},{7,8},{8,9},{9,10},{10,1... | collective-permute-start | bytes 393224 | tf_op jit(solution)/shard_map/ppermute | solution.py:26
  16.9 4.4 %add_divide_fusion.5 = f32[2,8,64,256]{3,2,1,0:T(8,128)S(1)} fusion(f32[2,8,64,256]{3,2,1,0:T(8,128)S(1)} %copy-done, f32[2,10,66,258]{3,2,1,0:T(8,128)S(1)} %select_maximum_fusion, f32[8,64,256]{2,1,0:T(8,128)S(1)} %get-tuple-element.32, f32[8,64,256]{2,1,0:T(8,128)S(1)} %copy-done.1, f32[2,1,64,256]{3,2,1,0:T(8,128)S(1)} %collective-permute-done.2, ...), kind=kLoop, calls=%fused_computation.670 | loop fusion | flops 15466496 | bytes 28573696 | tf_op jit(solution)/shard_map/div | solution.py:82
  34.3 4.7 %fusion.373 = (f32[3,2,8,64,256]{4,3,2,1,0:T(8,128)}, f32[3,2,8,64,256]{4,3,2,1,0:T(8,128)S(1)}) fusion(f32[3,2,8,64,256]{4,3,2,1,0:T(8,128)S(1)} %fusion.4), kind=kLoop, calls=%fused_computation.707 | loop fusion | flops 7077888 | bytes 9437184 | tf_op jit(solution)/shard_map/tanh | solution.py:124
  39.1 6.9 %add_divide_fusion.4 = f32[2,8,64,256]{3,2,1,0:T(8,128)S(1)} fusion(f32[2,8,64,256]{3,2,1,0:T(8,128)S(1)} %copy-done, f32[3,2,8,64,256]{4,3,2,1,0:T(8,128)} %get-tuple-element.14, f32[2,10,66,258]{3,2,1,0:T(8,128)S(1)} %select_maximum_fusion, f32[8,64,256]{2,1,0:T(8,128)S(1)} %get-tuple-element.32, f32[8,64,256]{2,1,0:T(8,128)S(1)} %copy-done.1, ...), kind=kLoop, calls=%fused_computation.669 | loop fusion | flops 27525120 | bytes 31719424 | tf_op jit(solution)/shard_map/div | solution.py:82
  46.6 15.6 %collective-permute-start.6 = (f32[3,2,2,64,256]{4,3,2,1,0:T(8,128)S(1)}, f32[3,2,2,64,256]{4,3,2,1,0:T(8,128)S(1)}, u32[]{:S(2)}, u32[]{:S(2)}) collective-permute-start(f32[3,2,2,64,256]{4,3,2,1,0:T(8,128)S(1)} %get-tuple-element.24), channel_id=1, source_target_pairs={{0,1},{1,2},{2,3},{3,4},{4,5},{5,6},{6,7},{7,8},{8,9},{9,10},{10,1... | collective-permute-start | bytes 2359304 | tf_op jit(solution)/shard_map/ppermute | solution.py:26
  64.1 4.3 %collective-permute-done.7 = f32[3,2,2,64,256]{4,3,2,1,0:T(8,128)S(1)} collective-permute-done((f32[3,2,2,64,256]{4,3,2,1,0:T(8,128)S(1)}, f32[3,2,2,64,256]{4,3,2,1,0:T(8,128)S(1)}, u32[]{:S(2)}, u32[]{:S(2)}) %collective-permute-start.7) | collective-permute-done | bytes 786464 | tf_op jit(solution)/shard_map/ppermute | solution.py:27
  72.1 4.7 %fusion.371 = (f32[3,2,8,64,256]{4,3,2,1,0:T(8,128)}, f32[3,2,8,64,256]{4,3,2,1,0:T(8,128)S(1)}) fusion(f32[3,2,8,64,256]{4,3,2,1,0:T(8,128)S(1)} %fusion.12), kind=kLoop, calls=%fused_computation.706 | loop fusion | flops 7077888 | bytes 9437184 | tf_op jit(solution)/shard_map/tanh | solution.py:124
  76.9 6.9 %add_divide_fusion.3 = f32[2,8,64,256]{3,2,1,0:T(8,128)S(1)} fusion(f32[2,8,64,256]{3,2,1,0:T(8,128)S(1)} %copy-done, f32[3,2,8,64,256]{4,3,2,1,0:T(8,128)} %get-tuple-element.12, f32[2,10,66,258]{3,2,1,0:T(8,128)S(1)} %select_maximum_fusion, f32[8,64,256]{2,1,0:T(8,128)S(1)} %get-tuple-element.32, f32[8,64,256]{2,1,0:T(8,128)S(1)} %copy-done.1, ...), kind=kLoop, calls=%fused_computation.668 | loop fusion | flops 27525120 | bytes 31719424 | tf_op jit(solution)/shard_map/div | solution.py:82
  84.4 15.6 %collective-permute-start.8 = (f32[3,2,2,64,256]{4,3,2,1,0:T(8,128)S(1)}, f32[3,2,2,64,256]{4,3,2,1,0:T(8,128)S(1)}, u32[]{:S(2)}, u32[]{:S(2)}) collective-permute-start(f32[3,2,2,64,256]{4,3,2,1,0:T(8,128)S(1)} %get-tuple-element.22), channel_id=1, source_target_pairs={{0,1},{1,2},{2,3},{3,4},{4,5},{5,6},{6,7},{7,8},{8,9},{9,10},{10,1... | collective-permute-start | bytes 2359304 | tf_op jit(solution)/shard_map/ppermute | solution.py:26
  101.9 4.3 %collective-permute-done.9 = f32[3,2,2,64,256]{4,3,2,1,0:T(8,128)S(1)} collective-permute-done((f32[3,2,2,64,256]{4,3,2,1,0:T(8,128)S(1)}, f32[3,2,2,64,256]{4,3,2,1,0:T(8,128)S(1)}, u32[]{:S(2)}, u32[]{:S(2)}) %collective-permute-start.9) | collective-permute-done | bytes 786464 | tf_op jit(solution)/shard_map/ppermute | solution.py:27
  110.1 4.7 %fusion.369 = (f32[3,2,8,64,256]{4,3,2,1,0:T(8,128)S(1)}, f32[3,2,8,64,256]{4,3,2,1,0:T(8,128)}) fusion(f32[3,2,8,64,256]{4,3,2,1,0:T(8,128)S(1)} %fusion.20), kind=kLoop, calls=%fused_computation.705 | loop fusion | flops 7077888 | bytes 9437184 | tf_op jit(solution)/shard_map/tanh | solution.py:128
  114.8 6.1 %fusion.367 = (f32[8,64,256]{2,1,0:T(8,128)S(1)}, f32[2,8,64,256]{3,2,1,0:T(8,128)}) fusion(f32[2,10,66,258]{3,2,1,0:T(8,128)S(1)} %select_maximum_fusion, f32[2,1,64,256]{3,2,1,0:T(8,128)S(1)} %collective-permute-done.3, f32[2,8,64,256]{3,2,1,0:T(8,128)S(1)} %copy-done, f32[2,1,64,256]{3,2,1,0:T(8,128)S(1)} %collective-permute-done.2, ...), kind=kLoop, calls=%fused_computation.704 | loop fusion | flops 26345472 | bytes 31195136 | tf_op jit(solution)/shard_map/reduce_sum | solution.py:129
  122.5 43.8 %psum.28 = f32[]{:T(128)} all-reduce(f32[]{:T(128)} %multiply_reduce_fusion.3), channel_id=1, replica_groups=mesh['group'=2,'brick'=16] {'brick'}, use_global_device_ids=true, to_apply=%region_2.3 | all-reduce | flops 1 | bytes 8 | tf_op jit(solution)/shard_map/psum | solution.py:107
  168.9 30.2 %psum.29 = f32[]{:T(128)} all-reduce(f32[]{:T(128)} %multiply_reduce_fusion.1), channel_id=1, replica_groups=mesh['group'=2,'brick'=16] {'brick'}, use_global_device_ids=true, to_apply=%region_4.5 | all-reduce | flops 1 | bytes 8 | tf_op jit(solution)/shard_map/psum | solution.py:109
  223.0 4.7 %fusion.365 = (f32[3,2,8,64,256]{4,3,2,1,0:T(8,128)}, f32[3,2,8,64,256]{4,3,2,1,0:T(8,128)S(1)}) fusion(f32[3,2,8,64,256]{4,3,2,1,0:T(8,128)S(1)} %fusion.28), kind=kLoop, calls=%fused_computation.703 | loop fusion | flops 7077888 | bytes 9437184 | tf_op jit(solution)/shard_map/tanh | solution.py:124
  227.7 6.9 %add_divide_fusion.1 = f32[2,8,64,256]{3,2,1,0:T(8,128)S(1)} fusion(f32[2,8,64,256]{3,2,1,0:T(8,128)S(1)} %copy-done, f32[3,2,8,64,256]{4,3,2,1,0:T(8,128)} %get-tuple-element.6, f32[2,10,66,258]{3,2,1,0:T(8,128)S(1)} %select_maximum_fusion, f32[8,64,256]{2,1,0:T(8,128)S(1)} %get-tuple-element.29, f32[8,64,256]{2,1,0:T(8,128)S(1)} %subtract_divide_fusion.1, ...), kind=kLoop, calls=%fused_computation.666 | loop fusion | flops 27525120 | bytes 31719424 | tf_op jit(solution)/shard_map/div | solution.py:82
  235.3 15.6 %collective-permute-start.14 = (f32[3,2,2,64,256]{4,3,2,1,0:T(8,128)S(1)}, f32[3,2,2,64,256]{4,3,2,1,0:T(8,128)S(1)}, u32[]{:S(2)}, u32[]{:S(2)}) collective-permute-start(f32[3,2,2,64,256]{4,3,2,1,0:T(8,128)S(1)} %get-tuple-element.18), channel_id=1, source_target_pairs={{0,1},{1,2},{2,3},{3,4},{4,5},{5,6},{6,7},{7,8},{8,9},{9,10},{10,1... | collective-permute-start | bytes 2359304 | tf_op jit(solution)/shard_map/ppermute | solution.py:26
  260.8 4.7 %fusion.363 = (f32[3,2,8,64,256]{4,3,2,1,0:T(8,128)}, f32[3,2,8,64,256]{4,3,2,1,0:T(8,128)S(1)}) fusion(f32[3,2,8,64,256]{4,3,2,1,0:T(8,128)S(1)} %fusion.36), kind=kLoop, calls=%fused_computation.702 | loop fusion | flops 7077888 | bytes 9437184 | tf_op jit(solution)/shard_map/tanh | solution.py:124
  265.5 6.9 %add_divide_fusion = f32[2,8,64,256]{3,2,1,0:T(8,128)S(1)} fusion(f32[2,8,64,256]{3,2,1,0:T(8,128)S(1)} %copy-done, f32[3,2,8,64,256]{4,3,2,1,0:T(8,128)} %get-tuple-element.4, f32[2,10,66,258]{3,2,1,0:T(8,128)S(1)} %select_maximum_fusion, f32[8,64,256]{2,1,0:T(8,128)S(1)} %get-tuple-element.29, f32[8,64,256]{2,1,0:T(8,128)S(1)} %subtract_divide_fusion.1, ...), kind=kLoop, calls=%fused_computation.665 | loop fusion | flops 27525120 | bytes 31719424 | tf_op jit(solution)/shard_map/div | solution.py:82
  273.1 13.6 %collective-permute-start.16 = (f32[3,2,2,64,256]{4,3,2,1,0:T(8,128)S(1)}, f32[3,2,2,64,256]{4,3,2,1,0:T(8,128)S(1)}, u32[]{:S(2)}, u32[]{:S(2)}) collective-permute-start(f32[3,2,2,64,256]{4,3,2,1,0:T(8,128)S(1)} %get-tuple-element.16), channel_id=1, source_target_pairs={{0,1},{1,2},{2,3},{3,4},{4,5},{5,6},{6,7},{7,8},{8,9},{9,10},{10,1... | collective-permute-start | bytes 2359304 | tf_op jit(solution)/shard_map/ppermute | solution.py:26
  296.7 4.7 %fusion.361 = (f32[3,2,8,64,256]{4,3,2,1,0:T(8,128)S(1)}, f32[3,2,8,64,256]{4,3,2,1,0:T(8,128)}) fusion(f32[3,2,8,64,256]{4,3,2,1,0:T(8,128)S(1)} %fusion.44), kind=kLoop, calls=%fused_computation.701 | loop fusion | flops 7077888 | bytes 9437184 | tf_op jit(solution)/shard_map/tanh | solution.py:128
  301.4 5.3 %fusion.163 = f32[8,64,256]{2,1,0:T(8,128)S(1)} fusion(f32[2,8,64,256]{3,2,1,0:T(8,128)S(1)} %copy-done, f32[3,2,8,64,256]{4,3,2,1,0:T(8,128)S(1)} %get-tuple-element.2, f32[2,10,66,258]{3,2,1,0:T(8,128)S(1)} %select_maximum_fusion, f32[2,1,64,256]{3,2,1,0:T(8,128)S(1)} %collective-permute-done.2, f32[2,1,64,256]{3,2,1,0:T(8,128)S(1)} %collective-permute-done.3), kind=kLoop, calls=%fused_computation.272 | loop fusion | flops 26345472 | bytes 30146560 | tf_op jit(solution)/shard_map/reduce_sum | solution.py:129
  308.2 40.4 %psum.30 = f32[]{:T(128)} all-reduce(f32[]{:T(128)} %multiply_reduce_fusion.2), channel_id=1, replica_groups=mesh['group'=2,'brick'=16] {'brick'}, use_global_device_ids=true, to_apply=%region_7.8 | all-reduce | flops 1 | bytes 8 | tf_op jit(solution)/shard_map/psum | solution.py:107
  351.1 30.1 %psum.31 = f32[]{:T(128)} all-reduce(f32[]{:T(128)} %multiply_reduce_fusion), channel_id=1, replica_groups=mesh['group'=2,'brick'=16] {'brick'}, use_global_device_ids=true, to_apply=%region_9.10 | all-reduce | flops 1 | bytes 8 | tf_op jit(solution)/shard_map/psum | solution.py:109
  (82 shorter events, 90.3 us)
Async XLA Ops:
  1.5 11.1 %collective-permute-start = (f32[1,64,256]{2,1,0:T(8,128)S(1)}, f32[1,64,256]{2,1,0:T(8,128)S(1)}, u32[]{:S(2)}, u32[]{:S(2)}) collective-permute-start(f32[1,64,256]{2,1,0:T(8,128)S(1)} %get-tuple-element.40), channel_id=1, source_target_pairs={{1,0},{2,1},{3,2},{4,3},{5,4},{6,5},{7,6},{8,7},{9,8},{10,9},{11,1... | collective-permute-start | bytes 196616 | tf_op jit(solution)/shard_map/ppermute | solution.py:27
  2.8 9.9 %collective-permute-start.1 = (f32[1,64,256]{2,1,0:T(8,128)S(1)}, f32[1,64,256]{2,1,0:T(8,128)S(1)}, u32[]{:S(2)}, u32[]{:S(2)}) collective-permute-start(f32[1,64,256]{2,1,0:T(8,128)S(1)} %get-tuple-element.41), channel_id=1, source_target_pairs={{0,1},{1,2},{2,3},{3,4},{4,5},{5,6},{6,7},{7,8},{8,9},{9,10},{10,1... | collective-permute-start | bytes 196616 | tf_op jit(solution)/shard_map/ppermute | solution.py:26
  6.9 9.1 %collective-permute-start.2 = (f32[2,1,64,256]{3,2,1,0:T(8,128)S(1)}, f32[2,1,64,256]{3,2,1,0:T(8,128)S(1)}, u32[]{:S(2)}, u32[]{:S(2)}) collective-permute-start(f32[2,1,64,256]{3,2,1,0:T(8,128)S(1)} %get-tuple-element.34), channel_id=1, source_target_pairs={{0,1},{1,2},{2,3},{3,4},{4,5},{5,6},{6,7},{7,8},{8,9},{9,10},{10,1... | collective-permute-start | bytes 393224 | tf_op jit(solution)/shard_map/ppermute | solution.py:26
  11.4 4.6 %collective-permute-start.3 = (f32[2,1,64,256]{3,2,1,0:T(8,128)S(1)}, f32[2,1,64,256]{3,2,1,0:T(8,128)S(1)}, u32[]{:S(2)}, u32[]{:S(2)}) collective-permute-start(f32[2,1,64,256]{3,2,1,0:T(8,128)S(1)} %get-tuple-element.35), channel_id=1, source_target_pairs={{1,0},{2,1},{3,2},{4,3},{5,4},{6,5},{7,6},{8,7},{9,8},{10,9},{11,1... | collective-permute-start | bytes 393224 | tf_op jit(solution)/shard_map/ppermute | solution.py:27
  14.1 1.9 copy-start
  15.9 1.0 copy-start.1
  21.8 6.0 %collective-permute-start.4 = (f32[3,2,2,64,256]{4,3,2,1,0:T(8,128)S(1)}, f32[3,2,2,64,256]{4,3,2,1,0:T(8,128)S(1)}, u32[]{:S(2)}, u32[]{:S(2)}) collective-permute-start(f32[3,2,2,64,256]{4,3,2,1,0:T(8,128)S(1)} %get-tuple-element.26), channel_id=1, source_target_pairs={{0,1},{1,2},{2,3},{3,4},{4,5},{5,6},{6,7},{7,8},{8,9},{9,10},{10,1... | collective-permute-start | bytes 2359304 | tf_op jit(solution)/shard_map/ppermute | solution.py:26
  26.0 4.5 %collective-permute-start.5 = (f32[3,2,2,64,256]{4,3,2,1,0:T(8,128)S(1)}, f32[3,2,2,64,256]{4,3,2,1,0:T(8,128)S(1)}, u32[]{:S(2)}, u32[]{:S(2)}) collective-permute-start(f32[3,2,2,64,256]{4,3,2,1,0:T(8,128)S(1)} %get-tuple-element.27), channel_id=1, source_target_pairs={{1,0},{2,1},{3,2},{4,3},{5,4},{6,5},{7,6},{8,7},{9,8},{10,9},{11,1... | collective-permute-start | bytes 2359304 | tf_op jit(solution)/shard_map/ppermute | solution.py:27
  46.6 17.5 %collective-permute-start.6 = (f32[3,2,2,64,256]{4,3,2,1,0:T(8,128)S(1)}, f32[3,2,2,64,256]{4,3,2,1,0:T(8,128)S(1)}, u32[]{:S(2)}, u32[]{:S(2)}) collective-permute-start(f32[3,2,2,64,256]{4,3,2,1,0:T(8,128)S(1)} %get-tuple-element.24), channel_id=1, source_target_pairs={{0,1},{1,2},{2,3},{3,4},{4,5},{5,6},{6,7},{7,8},{8,9},{9,10},{10,1... | collective-permute-start | bytes 2359304 | tf_op jit(solution)/shard_map/ppermute | solution.py:26
  62.2 6.1 %collective-permute-start.7 = (f32[3,2,2,64,256]{4,3,2,1,0:T(8,128)S(1)}, f32[3,2,2,64,256]{4,3,2,1,0:T(8,128)S(1)}, u32[]{:S(2)}, u32[]{:S(2)}) collective-permute-start(f32[3,2,2,64,256]{4,3,2,1,0:T(8,128)S(1)} %get-tuple-element.25), channel_id=1, source_target_pairs={{1,0},{2,1},{3,2},{4,3},{5,4},{6,5},{7,6},{8,7},{9,8},{10,9},{11,1... | collective-permute-start | bytes 2359304 | tf_op jit(solution)/shard_map/ppermute | solution.py:27
  84.4 17.5 %collective-permute-start.8 = (f32[3,2,2,64,256]{4,3,2,1,0:T(8,128)S(1)}, f32[3,2,2,64,256]{4,3,2,1,0:T(8,128)S(1)}, u32[]{:S(2)}, u32[]{:S(2)}) collective-permute-start(f32[3,2,2,64,256]{4,3,2,1,0:T(8,128)S(1)} %get-tuple-element.22), channel_id=1, source_target_pairs={{0,1},{1,2},{2,3},{3,4},{4,5},{5,6},{6,7},{7,8},{8,9},{9,10},{10,1... | collective-permute-start | bytes 2359304 | tf_op jit(solution)/shard_map/ppermute | solution.py:26
  100.1 6.1 %collective-permute-start.9 = (f32[3,2,2,64,256]{4,3,2,1,0:T(8,128)S(1)}, f32[3,2,2,64,256]{4,3,2,1,0:T(8,128)S(1)}, u32[]{:S(2)}, u32[]{:S(2)}) collective-permute-start(f32[3,2,2,64,256]{4,3,2,1,0:T(8,128)S(1)} %get-tuple-element.23), channel_id=1, source_target_pairs={{1,0},{2,1},{3,2},{4,3},{5,4},{6,5},{7,6},{8,7},{9,8},{10,9},{11,1... | collective-permute-start | bytes 2359304 | tf_op jit(solution)/shard_map/ppermute | solution.py:27
  120.9 0.8 copy-start.4
  200.9 4.5 %collective-permute-start.10 = (f32[1,64,256]{2,1,0:T(8,128)S(1)}, f32[1,64,256]{2,1,0:T(8,128)S(1)}, u32[]{:S(2)}, u32[]{:S(2)}) collective-permute-start(f32[1,64,256]{2,1,0:T(8,128)S(1)} %get-tuple-element.38), channel_id=1, source_target_pairs={{1,0},{2,1},{3,2},{4,3},{5,4},{6,5},{7,6},{8,7},{9,8},{10,9},{11,1... | collective-permute-start | bytes 196616 | tf_op jit(solution)/shard_map/ppermute | solution.py:27
  202.2 5.0 %copy-start.5 = (f32[2,8,64,256]{3,2,1,0:T(8,128)S(1)}, f32[2,8,64,256]{3,2,1,0:T(8,128)}, u32[]{:S(2)}) copy-start(f32[2,8,64,256]{3,2,1,0:T(8,128)} %get-tuple-element.9) | copy-start | bytes 3145732
  202.2 4.1 %collective-permute-start.11 = (f32[1,64,256]{2,1,0:T(8,128)S(1)}, f32[1,64,256]{2,1,0:T(8,128)S(1)}, u32[]{:S(2)}, u32[]{:S(2)}) collective-permute-start(f32[1,64,256]{2,1,0:T(8,128)S(1)} %get-tuple-element.39), channel_id=1, source_target_pairs={{0,1},{1,2},{2,3},{3,4},{4,5},{5,6},{6,7},{7,8},{8,9},{9,10},{10,1... | collective-permute-start | bytes 196616 | tf_op jit(solution)/shard_map/ppermute | solution.py:26
  207.2 1.9 copy-start.2
  209.7 5.3 %collective-permute-start.12 = (f32[3,2,2,64,256]{4,3,2,1,0:T(8,128)S(1)}, f32[3,2,2,64,256]{4,3,2,1,0:T(8,128)S(1)}, u32[]{:S(2)}, u32[]{:S(2)}) collective-permute-start(f32[3,2,2,64,256]{4,3,2,1,0:T(8,128)S(1)} %get-tuple-element.20), channel_id=1, source_target_pairs={{0,1},{1,2},{2,3},{3,4},{4,5},{5,6},{6,7},{7,8},{8,9},{9,10},{10,1... | collective-permute-start | bytes 2359304 | tf_op jit(solution)/shard_map/ppermute | solution.py:26
  213.2 6.0 %collective-permute-start.13 = (f32[3,2,2,64,256]{4,3,2,1,0:T(8,128)S(1)}, f32[3,2,2,64,256]{4,3,2,1,0:T(8,128)S(1)}, u32[]{:S(2)}, u32[]{:S(2)}) collective-permute-start(f32[3,2,2,64,256]{4,3,2,1,0:T(8,128)S(1)} %get-tuple-element.21), channel_id=1, source_target_pairs={{1,0},{2,1},{3,2},{4,3},{5,4},{6,5},{7,6},{8,7},{9,8},{10,9},{11,1... | collective-permute-start | bytes 2359304 | tf_op jit(solution)/shard_map/ppermute | solution.py:27
  235.3 17.5 %collective-permute-start.14 = (f32[3,2,2,64,256]{4,3,2,1,0:T(8,128)S(1)}, f32[3,2,2,64,256]{4,3,2,1,0:T(8,128)S(1)}, u32[]{:S(2)}, u32[]{:S(2)}) collective-permute-start(f32[3,2,2,64,256]{4,3,2,1,0:T(8,128)S(1)} %get-tuple-element.18), channel_id=1, source_target_pairs={{0,1},{1,2},{2,3},{3,4},{4,5},{5,6},{6,7},{7,8},{8,9},{9,10},{10,1... | collective-permute-start | bytes 2359304 | tf_op jit(solution)/shard_map/ppermute | solution.py:26
  250.9 6.1 %collective-permute-start.15 = (f32[3,2,2,64,256]{4,3,2,1,0:T(8,128)S(1)}, f32[3,2,2,64,256]{4,3,2,1,0:T(8,128)S(1)}, u32[]{:S(2)}, u32[]{:S(2)}) collective-permute-start(f32[3,2,2,64,256]{4,3,2,1,0:T(8,128)S(1)} %get-tuple-element.19), channel_id=1, source_target_pairs={{1,0},{2,1},{3,2},{4,3},{5,4},{6,5},{7,6},{8,7},{9,8},{10,9},{11,1... | collective-permute-start | bytes 2359304 | tf_op jit(solution)/shard_map/ppermute | solution.py:27
  273.1 15.4 %collective-permute-start.16 = (f32[3,2,2,64,256]{4,3,2,1,0:T(8,128)S(1)}, f32[3,2,2,64,256]{4,3,2,1,0:T(8,128)S(1)}, u32[]{:S(2)}, u32[]{:S(2)}) collective-permute-start(f32[3,2,2,64,256]{4,3,2,1,0:T(8,128)S(1)} %get-tuple-element.16), channel_id=1, source_target_pairs={{0,1},{1,2},{2,3},{3,4},{4,5},{5,6},{6,7},{7,8},{8,9},{9,10},{10,1... | collective-permute-start | bytes 2359304 | tf_op jit(solution)/shard_map/ppermute | solution.py:26
  286.7 6.1 %collective-permute-start.17 = (f32[3,2,2,64,256]{4,3,2,1,0:T(8,128)S(1)}, f32[3,2,2,64,256]{4,3,2,1,0:T(8,128)S(1)}, u32[]{:S(2)}, u32[]{:S(2)}) collective-permute-start(f32[3,2,2,64,256]{4,3,2,1,0:T(8,128)S(1)} %get-tuple-element.17), channel_id=1, source_target_pairs={{1,0},{2,1},{3,2},{4,3},{5,4},{6,5},{7,6},{8,7},{9,8},{10,9},{11,1... | collective-permute-start | bytes 2359304 | tf_op jit(solution)/shard_map/ppermute | solution.py:27
  306.7 0.8 copy-start.3
where the time goes:
time: 389 us; the launch traced here: 384 us
  blocking collectives  145 us (37%)
  other arithmetic  111 us (29%)
  starting transfers between devices  92.1 us (24%)
  waiting for transfers between devices  26.3 us (7%)
  local copies, waits for them, and re-layouts  5.91 us (2%)
  between operations  4.45 us (1%)
    psum x2, blocking collectives, normalize(): mu = lax.psum(jnp.sum(mean_image), 'brick') / count  84.2 us
    ppermute x9, starting transfers between devices, padded_2(): before = lax.ppermute(last, axis, up)  78.7 us
    psum x2, blocking collectives, normalize(): var = lax.psum(jnp.sum(centered * centered), 'brick') / count  60.3 us
    div x6, other arithmetic, forces(): ratio = STEP * diff / denom  32.1 us
    tanh x6, other arithmetic, per_device(): warped = warp_image(image_pad, jnp.tanh(fields))  28.3 us
    ppermute x9, waiting for transfers between devices, padded_2(): after = lax.ppermute(initial, axis, down)  23.9 us
    ppermute x9, starting transfers between devices, padded_2(): after = lax.ppermute(initial, axis, down)  13.4 us
    add x6, other arithmetic, first_pass(): result + taps[k] * lax.slice_in_dim(extended, k, k + planes, axis=2)  11.5 us
  transfers between devices with their start and end apart: 18, of which 12 were waited for; matrix products, arithmetic and copies ran while one was open for 1% of the time, Pallas kernels for 0%

commit v1 on v0

--- a/solution.py
+++ b/solution.py
@@ -3,6 +3,8 @@
 import jax
 import jax.numpy as jnp
 from jax import lax
+from jax.experimental import pallas as pl
+from jax.experimental.pallas import tpu as pltpu
 from jax.sharding import PartitionSpec as P
 
 RAD = 2
@@ -103,11 +105,57 @@
     return result
 
 
+def gather_kernel(n, x_ref, o_ref, send_sem, recv_sem):
+    me = lax.axis_index("brick")
+    barrier = pltpu.get_barrier_semaphore()
+    for k in range(1, n):
+        pl.semaphore_signal(
+            barrier, inc=1, device_id={"brick": lax.rem(me + k, n)},
+            device_id_type=pl.DeviceIdType.MESH,
+        )
+    pl.semaphore_wait(barrier, n - 1)
+    copies = []
+    for k in range(1, n):
+        copy = pltpu.make_async_remote_copy(
+            src_ref=x_ref,
+            dst_ref=o_ref.at[k],
+            send_sem=send_sem.at[k],
+            recv_sem=recv_sem.at[k],
+            device_id={"brick": lax.rem(me + k, n)},
+            device_id_type=pl.DeviceIdType.MESH,
+        )
+        copy.start()
+        copies.append(copy)
+    o_ref[0] = x_ref[...]
+    for copy in copies:
+        copy.wait()
+
+
+def gather_tiles(tile, n):
+    return pl.pallas_call(
+        lambda *refs: gather_kernel(n, *refs),
+        out_shape=jax.ShapeDtypeStruct((n,) + tile.shape, tile.dtype),
+        in_specs=[pl.BlockSpec(memory_space=pltpu.VMEM)],
+        out_specs=pl.BlockSpec(memory_space=pltpu.VMEM),
+        scratch_shapes=[pltpu.SemaphoreType.DMA((n,)), pltpu.SemaphoreType.DMA((n,))],
+        compiler_params=pltpu.CompilerParams(collective_id=0, has_side_effects=True),
+    )(tile)
+
+
 def normalize(mean_image, count):
-    mu = lax.psum(jnp.sum(mean_image), "brick") / count
-    centered = mean_image - mu
-    var = lax.psum(jnp.sum(centered * centered), "brick") / count
-    return centered / jnp.sqrt(var + EPS)
+    n = lax.axis_size("brick")
+    own = count // n
+    total = jnp.sum(mean_image)
+    away = mean_image - total / own
+    spread = jnp.sum(away * away)
+    lane = lax.broadcasted_iota(jnp.int32, (8, 128), 1)
+    tile = jnp.where(lane == 0, total, jnp.where(lane == 1, spread, 0.0))
+    every = gather_tiles(tile, n)
+    totals, spreads = every[:, 0, 0], every[:, 0, 1]
+    mu = jnp.sum(totals) / count
+    offsets = totals / own - mu
+    var = (jnp.sum(spreads) + own * jnp.sum(offsets * offsets)) / count
+    return (mean_image - mu) / jnp.sqrt(var + EPS)
 
 
 def per_device(subjects, template):

time: 389 us -> 316 us (0.81)
  blocking collectives: 145 us -> 0 us
  Pallas kernels: 0 us -> 46.3 us
  other arithmetic: 111 us -> 130 us
    psum x4 -> x0, blocking collectives: 145 us -> none  [the longest x2 84.2 us: normalize(): mu = lax.psum(jnp.sum(mean_image), 'brick') / count]
    pallas_call x0 -> x2, Pallas kernels: none -> 46.3 us  [gather_tiles(): pl.pallas_call(lambda *refs: gather_kernel(n, *refs), out_shape=jax.Shape...]
    add x5, other arithmetic: 2.66 us -> 9.99 us  [forces(): return state + grads[:, None] * ratio[None]]
    reduce_sum x4 -> x8, other arithmetic: 5.23 us -> 11.5 us  [the longest x2 3.62 us: normalize(): spread = jnp.sum(away * away)]
where the time goes in v1:
time: 316 us; the launch traced here: 310 us
  other arithmetic  130 us (41%)
  starting transfers between devices  94.4 us (30%)
  Pallas kernels  46.3 us (15%)
  waiting for transfers between devices  26.3 us (8%)
  between operations  7.02 us (2%)
  local copies, waits for them, and re-layouts  6.22 us (2%)
    ppermute x9, starting transfers between devices, padded_2(): before = lax.ppermute(last, axis, up)  81 us
    pallas_call x2, Pallas kernels, gather_tiles(): pl.pallas_call(lambda *refs: gather_kernel(n, *refs), out_shape=jax.Shape...  46.3 us
    div x6, other arithmetic, forces(): ratio = STEP * diff / denom  32.9 us
    tanh x6, other arithmetic, per_device(): warped = warp_image(image_pad, jnp.tanh(fields))  29.9 us
    ppermute x9, waiting for transfers between devices, padded_2(): after = lax.ppermute(initial, axis, down)  24 us
    ppermute x9, starting transfers between devices, padded_2(): after = lax.ppermute(initial, axis, down)  13.4 us
    add x6, other arithmetic, along_axis(): result + taps[k] * lax.slice_in_dim(padded, k, k + size_here, axis=axis)  11.5 us
    reduce_sum x2, other arithmetic, per_device(): current = normalize(jnp.mean(warped, axis=0), count)  11.3 us
  transfers between devices with their start and end apart: 18, of which 12 were waited for; matrix products, arithmetic and copies ran while one was open for 1% of the time, Pallas kernels for 0%

profile of v1, /device:TPU:0, one launch (start us, length us, event | category | flops | bytes accessed | tf_op | source)
XLA Modules:
  0.0 310.2 jit_solution(12731836525054959123)
XLA Ops:
  6.9 4.5 %collective-permute-start.2 = (f32[2,1,64,256]{3,2,1,0:T(8,128)S(1)}, f32[2,1,64,256]{3,2,1,0:T(8,128)S(1)}, u32[]{:S(2)}, u32[]{:S(2)}) collective-permute-start(f32[2,1,64,256]{3,2,1,0:T(8,128)S(1)} %get-tuple-element.38), channel_id=1, source_target_pairs={{0,1},{1,2},{2,3},{3,4},{4,5},{5,6},{6,7},{7,8},{8,9},{9,10},{10,1... | collective-permute-start | bytes 393224 | tf_op jit(solution)/shard_map/ppermute | solution.py:28
  16.9 4.4 %add_divide_fusion.5 = f32[2,8,64,256]{3,2,1,0:T(8,128)S(1)} fusion(f32[2,8,64,256]{3,2,1,0:T(8,128)S(1)} %copy-done, f32[2,10,66,258]{3,2,1,0:T(8,128)S(1)} %select_maximum_fusion, f32[8,64,256]{2,1,0:T(8,128)S(1)} %get-tuple-element.36, f32[8,64,256]{2,1,0:T(8,128)S(1)} %copy-done.1, f32[2,1,64,256]{3,2,1,0:T(8,128)S(1)} %collective-permute-done.2, ...), kind=kLoop, calls=%fused_computation.670 | loop fusion | flops 15466496 | bytes 28573696 | tf_op jit(solution)/shard_map/div | solution.py:84
  34.4 5.3 %fusion.373 = (f32[3,2,8,64,256]{4,3,2,1,0:T(8,128)}, f32[3,2,8,64,256]{4,3,2,1,0:T(8,128)}) fusion(f32[3,2,8,64,256]{4,3,2,1,0:T(8,128)S(1)} %fusion.4), kind=kLoop, calls=%fused_computation.718 | loop fusion | flops 7077888 | bytes 9437184 | tf_op jit(solution)/shard_map/tanh | solution.py:172
  39.6 6.9 %add_divide_fusion.4 = f32[2,8,64,256]{3,2,1,0:T(8,128)S(1)} fusion(f32[2,8,64,256]{3,2,1,0:T(8,128)S(1)} %copy-done, f32[3,2,8,64,256]{4,3,2,1,0:T(8,128)} %get-tuple-element.18, f32[2,10,66,258]{3,2,1,0:T(8,128)S(1)} %select_maximum_fusion, f32[8,64,256]{2,1,0:T(8,128)S(1)} %get-tuple-element.36, f32[8,64,256]{2,1,0:T(8,128)S(1)} %copy-done.1, ...), kind=kLoop, calls=%fused_computation.669 | loop fusion | flops 27525120 | bytes 31719424 | tf_op jit(solution)/shard_map/div | solution.py:84
  49.1 15.6 %collective-permute-start.6 = (f32[3,2,2,64,256]{4,3,2,1,0:T(8,128)S(1)}, f32[3,2,2,64,256]{4,3,2,1,0:T(8,128)S(1)}, u32[]{:S(2)}, u32[]{:S(2)}) collective-permute-start(f32[3,2,2,64,256]{4,3,2,1,0:T(8,128)S(1)} %get-tuple-element.28), channel_id=1, source_target_pairs={{0,1},{1,2},{2,3},{3,4},{4,5},{5,6},{6,7},{7,8},{8,9},{9,10},{10,1... | collective-permute-start | bytes 2359304 | tf_op jit(solution)/shard_map/ppermute | solution.py:28
  66.5 4.3 %collective-permute-done.7 = f32[3,2,2,64,256]{4,3,2,1,0:T(8,128)S(1)} collective-permute-done((f32[3,2,2,64,256]{4,3,2,1,0:T(8,128)S(1)}, f32[3,2,2,64,256]{4,3,2,1,0:T(8,128)S(1)}, u32[]{:S(2)}, u32[]{:S(2)}) %collective-permute-start.7) | collective-permute-done | bytes 786464 | tf_op jit(solution)/shard_map/ppermute | solution.py:29
  74.5 5.3 %fusion.371 = (f32[3,2,8,64,256]{4,3,2,1,0:T(8,128)}, f32[3,2,8,64,256]{4,3,2,1,0:T(8,128)}) fusion(f32[3,2,8,64,256]{4,3,2,1,0:T(8,128)S(1)} %fusion.12), kind=kLoop, calls=%fused_computation.717 | loop fusion | flops 7077888 | bytes 9437184 | tf_op jit(solution)/shard_map/tanh | solution.py:172
  79.7 6.9 %add_divide_fusion.3 = f32[2,8,64,256]{3,2,1,0:T(8,128)S(1)} fusion(f32[2,8,64,256]{3,2,1,0:T(8,128)S(1)} %copy-done, f32[3,2,8,64,256]{4,3,2,1,0:T(8,128)} %get-tuple-element.16, f32[2,10,66,258]{3,2,1,0:T(8,128)S(1)} %select_maximum_fusion, f32[8,64,256]{2,1,0:T(8,128)S(1)} %get-tuple-element.36, f32[8,64,256]{2,1,0:T(8,128)S(1)} %copy-done.1, ...), kind=kLoop, calls=%fused_computation.668 | loop fusion | flops 27525120 | bytes 31719424 | tf_op jit(solution)/shard_map/div | solution.py:84
  89.2 15.6 %collective-permute-start.8 = (f32[3,2,2,64,256]{4,3,2,1,0:T(8,128)S(1)}, f32[3,2,2,64,256]{4,3,2,1,0:T(8,128)S(1)}, u32[]{:S(2)}, u32[]{:S(2)}) collective-permute-start(f32[3,2,2,64,256]{4,3,2,1,0:T(8,128)S(1)} %get-tuple-element.26), channel_id=1, source_target_pairs={{0,1},{1,2},{2,3},{3,4},{4,5},{5,6},{6,7},{7,8},{8,9},{9,10},{10,1... | collective-permute-start | bytes 2359304 | tf_op jit(solution)/shard_map/ppermute | solution.py:28
  106.7 4.3 %collective-permute-done.9 = f32[3,2,2,64,256]{4,3,2,1,0:T(8,128)S(1)} collective-permute-done((f32[3,2,2,64,256]{4,3,2,1,0:T(8,128)S(1)}, f32[3,2,2,64,256]{4,3,2,1,0:T(8,128)S(1)}, u32[]{:S(2)}, u32[]{:S(2)}) %collective-permute-start.9) | collective-permute-done | bytes 786464 | tf_op jit(solution)/shard_map/ppermute | solution.py:29
  114.7 4.7 %fusion.369 = (f32[3,2,8,64,256]{4,3,2,1,0:T(8,128)S(1)}, f32[3,2,8,64,256]{4,3,2,1,0:T(8,128)}) fusion(f32[3,2,8,64,256]{4,3,2,1,0:T(8,128)S(1)} %fusion.20), kind=kLoop, calls=%fused_computation.716 | loop fusion | flops 7077888 | bytes 9437184 | tf_op jit(solution)/shard_map/tanh | solution.py:176
  119.5 6.1 %fusion.367 = (f32[8,64,256]{2,1,0:T(8,128)S(1)}, f32[2,8,64,256]{3,2,1,0:T(8,128)}) fusion(f32[2,10,66,258]{3,2,1,0:T(8,128)S(1)} %select_maximum_fusion, f32[2,1,64,256]{3,2,1,0:T(8,128)S(1)} %collective-permute-done.3, f32[2,8,64,256]{3,2,1,0:T(8,128)S(1)} %copy-done, f32[2,1,64,256]{3,2,1,0:T(8,128)S(1)} %collective-permute-done.2, ...), kind=kLoop, calls=%fused_computation.715 | loop fusion | flops 26345472 | bytes 31195136 | tf_op jit(solution)/shard_map/reduce_sum | solution.py:177
  131.3 22.7 %shard_map.41 = f32[16,8,128]{2,1,0:T(8,128)} custom-call(f32[8,128]{1,0:T(8,128)} %broadcast_select_fusion.1.refs_0_), custom_call_target="tpu_custom_call" | custom-call | tf_op jit(solution)/shard_map/pallas_call | solution.py:135
  183.1 5.3 %fusion.365 = (f32[3,2,8,64,256]{4,3,2,1,0:T(8,128)}, f32[3,2,8,64,256]{4,3,2,1,0:T(8,128)}) fusion(f32[3,2,8,64,256]{4,3,2,1,0:T(8,128)S(1)} %fusion.28), kind=kLoop, calls=%fused_computation.714 | loop fusion | flops 7077888 | bytes 9437184 | tf_op jit(solution)/shard_map/tanh | solution.py:172
  188.4 6.9 %add_divide_fusion.1 = f32[2,8,64,256]{3,2,1,0:T(8,128)S(1)} fusion(f32[2,8,64,256]{3,2,1,0:T(8,128)S(1)} %copy-done, f32[3,2,8,64,256]{4,3,2,1,0:T(8,128)} %get-tuple-element.10, f32[2,10,66,258]{3,2,1,0:T(8,128)S(1)} %select_maximum_fusion, f32[8,64,256]{2,1,0:T(8,128)S(1)} %get-tuple-element.33, f32[8,64,256]{2,1,0:T(8,128)S(1)} %subtract_divide_fusion.1, ...), kind=kLoop, calls=%fused_computation.666 | loop fusion | flops 27525120 | bytes 31719424 | tf_op jit(solution)/shard_map/div | solution.py:84
  197.9 15.6 %collective-permute-start.14 = (f32[3,2,2,64,256]{4,3,2,1,0:T(8,128)S(1)}, f32[3,2,2,64,256]{4,3,2,1,0:T(8,128)S(1)}, u32[]{:S(2)}, u32[]{:S(2)}) collective-permute-start(f32[3,2,2,64,256]{4,3,2,1,0:T(8,128)S(1)} %get-tuple-element.22), channel_id=1, source_target_pairs={{0,1},{1,2},{2,3},{3,4},{4,5},{5,6},{6,7},{7,8},{8,9},{9,10},{10,1... | collective-permute-start | bytes 2359304 | tf_op jit(solution)/shard_map/ppermute | solution.py:28
  215.3 4.3 %collective-permute-done.15 = f32[3,2,2,64,256]{4,3,2,1,0:T(8,128)S(1)} collective-permute-done((f32[3,2,2,64,256]{4,3,2,1,0:T(8,128)S(1)}, f32[3,2,2,64,256]{4,3,2,1,0:T(8,128)S(1)}, u32[]{:S(2)}, u32[]{:S(2)}) %collective-permute-start.15) | collective-permute-done | bytes 786464 | tf_op jit(solution)/shard_map/ppermute | solution.py:29
  223.3 4.7 %fusion.363 = (f32[3,2,8,64,256]{4,3,2,1,0:T(8,128)}, f32[3,2,8,64,256]{4,3,2,1,0:T(8,128)S(1)}) fusion(f32[3,2,8,64,256]{4,3,2,1,0:T(8,128)S(1)} %fusion.36), kind=kLoop, calls=%fused_computation.713 | loop fusion | flops 7077888 | bytes 9437184 | tf_op jit(solution)/shard_map/tanh | solution.py:172
  228.0 7.6 %add_divide_fusion = f32[2,8,64,256]{3,2,1,0:T(8,128)} fusion(f32[2,8,64,256]{3,2,1,0:T(8,128)S(1)} %copy-done, f32[3,2,8,64,256]{4,3,2,1,0:T(8,128)} %get-tuple-element.8, f32[2,10,66,258]{3,2,1,0:T(8,128)S(1)} %select_maximum_fusion, f32[8,64,256]{2,1,0:T(8,128)S(1)} %copy-done.4, f32[8,64,256]{2,1,0:T(8,128)S(1)} %subtract_divide_fusion.1, ...), kind=kLoop, calls=%fused_computation.665 | loop fusion | flops 27525120 | bytes 31719424 | tf_op jit(solution)/shard_map/div | solution.py:84
  237.7 15.6 %collective-permute-start.16 = (f32[3,2,2,64,256]{4,3,2,1,0:T(8,128)S(1)}, f32[3,2,2,64,256]{4,3,2,1,0:T(8,128)S(1)}, u32[]{:S(2)}, u32[]{:S(2)}) collective-permute-start(f32[3,2,2,64,256]{4,3,2,1,0:T(8,128)S(1)} %get-tuple-element.20), channel_id=1, source_target_pairs={{0,1},{1,2},{2,3},{3,4},{4,5},{5,6},{6,7},{7,8},{8,9},{9,10},{10,1... | collective-permute-start | bytes 2359304 | tf_op jit(solution)/shard_map/ppermute | solution.py:28
  255.2 4.3 %collective-permute-done.17 = f32[3,2,2,64,256]{4,3,2,1,0:T(8,128)S(1)} collective-permute-done((f32[3,2,2,64,256]{4,3,2,1,0:T(8,128)S(1)}, f32[3,2,2,64,256]{4,3,2,1,0:T(8,128)S(1)}, u32[]{:S(2)}, u32[]{:S(2)}) %collective-permute-start.17) | collective-permute-done | bytes 786464 | tf_op jit(solution)/shard_map/ppermute | solution.py:29
  263.3 4.7 %fusion.361 = (f32[3,2,8,64,256]{4,3,2,1,0:T(8,128)S(1)}, f32[3,2,8,64,256]{4,3,2,1,0:T(8,128)}) fusion(f32[3,2,8,64,256]{4,3,2,1,0:T(8,128)S(1)} %fusion.44), kind=kLoop, calls=%fused_computation.712 | loop fusion | flops 7077888 | bytes 9437184 | tf_op jit(solution)/shard_map/tanh | solution.py:176
  268.0 5.3 %fusion.163 = f32[8,64,256]{2,1,0:T(8,128)S(1)} fusion(f32[2,8,64,256]{3,2,1,0:T(8,128)S(1)} %copy-done, f32[3,2,8,64,256]{4,3,2,1,0:T(8,128)S(1)} %get-tuple-element.6, f32[2,10,66,258]{3,2,1,0:T(8,128)S(1)} %select_maximum_fusion, f32[2,1,64,256]{3,2,1,0:T(8,128)S(1)} %collective-permute-done.2, f32[2,1,64,256]{3,2,1,0:T(8,128)S(1)} %collective-permute-done.3), kind=kLoop, calls=%fused_computation.272 | loop fusion | flops 26345472 | bytes 30146560 | tf_op jit(solution)/shard_map/reduce_sum | solution.py:177
  279.2 23.5 %shard_map.42 = f32[16,8,128]{2,1,0:T(8,128)} custom-call(f32[8,128]{1,0:T(8,128)} %broadcast_select_fusion.refs_0_), custom_call_target="tpu_custom_call" | custom-call | tf_op jit(solution)/shard_map/pallas_call | solution.py:135
  (93 shorter events, 99.0 us)
Async XLA Ops:
  1.5 11.1 %collective-permute-start = (f32[1,64,256]{2,1,0:T(8,128)S(1)}, f32[1,64,256]{2,1,0:T(8,128)S(1)}, u32[]{:S(2)}, u32[]{:S(2)}) collective-permute-start(f32[1,64,256]{2,1,0:T(8,128)S(1)} %get-tuple-element.44), channel_id=1, source_target_pairs={{1,0},{2,1},{3,2},{4,3},{5,4},{6,5},{7,6},{8,7},{9,8},{10,9},{11,1... | collective-permute-start | bytes 196616 | tf_op jit(solution)/shard_map/ppermute | solution.py:29
  2.8 9.9 %collective-permute-start.1 = (f32[1,64,256]{2,1,0:T(8,128)S(1)}, f32[1,64,256]{2,1,0:T(8,128)S(1)}, u32[]{:S(2)}, u32[]{:S(2)}) collective-permute-start(f32[1,64,256]{2,1,0:T(8,128)S(1)} %get-tuple-element.45), channel_id=1, source_target_pairs={{0,1},{1,2},{2,3},{3,4},{4,5},{5,6},{6,7},{7,8},{8,9},{9,10},{10,1... | collective-permute-start | bytes 196616 | tf_op jit(solution)/shard_map/ppermute | solution.py:28
  6.9 9.2 %collective-permute-start.2 = (f32[2,1,64,256]{3,2,1,0:T(8,128)S(1)}, f32[2,1,64,256]{3,2,1,0:T(8,128)S(1)}, u32[]{:S(2)}, u32[]{:S(2)}) collective-permute-start(f32[2,1,64,256]{3,2,1,0:T(8,128)S(1)} %get-tuple-element.38), channel_id=1, source_target_pairs={{0,1},{1,2},{2,3},{3,4},{4,5},{5,6},{6,7},{7,8},{8,9},{9,10},{10,1... | collective-permute-start | bytes 393224 | tf_op jit(solution)/shard_map/ppermute | solution.py:28
  11.4 4.7 %collective-permute-start.3 = (f32[2,1,64,256]{3,2,1,0:T(8,128)S(1)}, f32[2,1,64,256]{3,2,1,0:T(8,128)S(1)}, u32[]{:S(2)}, u32[]{:S(2)}) collective-permute-start(f32[2,1,64,256]{3,2,1,0:T(8,128)S(1)} %get-tuple-element.39), channel_id=1, source_target_pairs={{1,0},{2,1},{3,2},{4,3},{5,4},{6,5},{7,6},{8,7},{9,8},{10,9},{11,1... | collective-permute-start | bytes 393224 | tf_op jit(solution)/shard_map/ppermute | solution.py:29
  14.1 2.0 copy-start
  15.9 1.0 copy-start.1
  22.0 6.0 %collective-permute-start.4 = (f32[3,2,2,64,256]{4,3,2,1,0:T(8,128)S(1)}, f32[3,2,2,64,256]{4,3,2,1,0:T(8,128)S(1)}, u32[]{:S(2)}, u32[]{:S(2)}) collective-permute-start(f32[3,2,2,64,256]{4,3,2,1,0:T(8,128)S(1)} %get-tuple-element.30), channel_id=1, source_target_pairs={{0,1},{1,2},{2,3},{3,4},{4,5},{5,6},{6,7},{7,8},{8,9},{9,10},{10,1... | collective-permute-start | bytes 2359304 | tf_op jit(solution)/shard_map/ppermute | solution.py:28
  26.1 4.6 %collective-permute-start.5 = (f32[3,2,2,64,256]{4,3,2,1,0:T(8,128)S(1)}, f32[3,2,2,64,256]{4,3,2,1,0:T(8,128)S(1)}, u32[]{:S(2)}, u32[]{:S(2)}) collective-permute-start(f32[3,2,2,64,256]{4,3,2,1,0:T(8,128)S(1)} %get-tuple-element.31), channel_id=1, source_target_pairs={{1,0},{2,1},{3,2},{4,3},{5,4},{6,5},{7,6},{8,7},{9,8},{10,9},{11,1... | collective-permute-start | bytes 2359304 | tf_op jit(solution)/shard_map/ppermute | solution.py:29
  49.1 17.5 %collective-permute-start.6 = (f32[3,2,2,64,256]{4,3,2,1,0:T(8,128)S(1)}, f32[3,2,2,64,256]{4,3,2,1,0:T(8,128)S(1)}, u32[]{:S(2)}, u32[]{:S(2)}) collective-permute-start(f32[3,2,2,64,256]{4,3,2,1,0:T(8,128)S(1)} %get-tuple-element.28), channel_id=1, source_target_pairs={{0,1},{1,2},{2,3},{3,4},{4,5},{5,6},{6,7},{7,8},{8,9},{9,10},{10,1... | collective-permute-start | bytes 2359304 | tf_op jit(solution)/shard_map/ppermute | solution.py:28
  64.7 6.1 %collective-permute-start.7 = (f32[3,2,2,64,256]{4,3,2,1,0:T(8,128)S(1)}, f32[3,2,2,64,256]{4,3,2,1,0:T(8,128)S(1)}, u32[]{:S(2)}, u32[]{:S(2)}) collective-permute-start(f32[3,2,2,64,256]{4,3,2,1,0:T(8,128)S(1)} %get-tuple-element.29), channel_id=1, source_target_pairs={{1,0},{2,1},{3,2},{4,3},{5,4},{6,5},{7,6},{8,7},{9,8},{10,9},{11,1... | collective-permute-start | bytes 2359304 | tf_op jit(solution)/shard_map/ppermute | solution.py:29
  89.2 17.5 %collective-permute-start.8 = (f32[3,2,2,64,256]{4,3,2,1,0:T(8,128)S(1)}, f32[3,2,2,64,256]{4,3,2,1,0:T(8,128)S(1)}, u32[]{:S(2)}, u32[]{:S(2)}) collective-permute-start(f32[3,2,2,64,256]{4,3,2,1,0:T(8,128)S(1)} %get-tuple-element.26), channel_id=1, source_target_pairs={{0,1},{1,2},{2,3},{3,4},{4,5},{5,6},{6,7},{7,8},{8,9},{9,10},{10,1... | collective-permute-start | bytes 2359304 | tf_op jit(solution)/shard_map/ppermute | solution.py:28
  104.8 6.1 %collective-permute-start.9 = (f32[3,2,2,64,256]{4,3,2,1,0:T(8,128)S(1)}, f32[3,2,2,64,256]{4,3,2,1,0:T(8,128)S(1)}, u32[]{:S(2)}, u32[]{:S(2)}) collective-permute-start(f32[3,2,2,64,256]{4,3,2,1,0:T(8,128)S(1)} %get-tuple-element.27), channel_id=1, source_target_pairs={{1,0},{2,1},{3,2},{4,3},{5,4},{6,5},{7,6},{8,7},{9,8},{10,9},{11,1... | collective-permute-start | bytes 2359304 | tf_op jit(solution)/shard_map/ppermute | solution.py:29
  160.5 4.5 %collective-permute-start.10 = (f32[1,64,256]{2,1,0:T(8,128)S(1)}, f32[1,64,256]{2,1,0:T(8,128)S(1)}, u32[]{:S(2)}, u32[]{:S(2)}) collective-permute-start(f32[1,64,256]{2,1,0:T(8,128)S(1)} %get-tuple-element.42), channel_id=1, source_target_pairs={{1,0},{2,1},{3,2},{4,3},{5,4},{6,5},{7,6},{8,7},{9,8},{10,9},{11,1... | collective-permute-start | bytes 196616 | tf_op jit(solution)/shard_map/ppermute | solution.py:29
  161.8 5.0 %copy-start.7 = (f32[2,8,64,256]{3,2,1,0:T(8,128)S(1)}, f32[2,8,64,256]{3,2,1,0:T(8,128)}, u32[]{:S(2)}) copy-start(f32[2,8,64,256]{3,2,1,0:T(8,128)} %get-tuple-element.13) | copy-start | bytes 3145732
  161.8 4.1 %collective-permute-start.11 = (f32[1,64,256]{2,1,0:T(8,128)S(1)}, f32[1,64,256]{2,1,0:T(8,128)S(1)}, u32[]{:S(2)}, u32[]{:S(2)}) collective-permute-start(f32[1,64,256]{2,1,0:T(8,128)S(1)} %get-tuple-element.43), channel_id=1, source_target_pairs={{0,1},{1,2},{2,3},{3,4},{4,5},{5,6},{6,7},{7,8},{8,9},{9,10},{10,1... | collective-permute-start | bytes 196616 | tf_op jit(solution)/shard_map/ppermute | solution.py:28
  166.7 21.7 %copy-start.3 = (f32[8,64,256]{2,1,0:T(8,128)}, f32[8,64,256]{2,1,0:T(8,128)S(1)}, u32[]{:S(2)}) copy-start(f32[8,64,256]{2,1,0:T(8,128)S(1)} %get-tuple-element.33) | copy-start | bytes 1572868
  166.7 2.1 copy-start.2
  169.7 5.6 %collective-permute-start.12 = (f32[3,2,2,64,256]{4,3,2,1,0:T(8,128)S(1)}, f32[3,2,2,64,256]{4,3,2,1,0:T(8,128)S(1)}, u32[]{:S(2)}, u32[]{:S(2)}) collective-permute-start(f32[3,2,2,64,256]{4,3,2,1,0:T(8,128)S(1)} %get-tuple-element.24), channel_id=1, source_target_pairs={{0,1},{1,2},{2,3},{3,4},{4,5},{5,6},{6,7},{7,8},{8,9},{9,10},{10,1... | collective-permute-start | bytes 2359304 | tf_op jit(solution)/shard_map/ppermute | solution.py:28
  173.5 6.0 %collective-permute-start.13 = (f32[3,2,2,64,256]{4,3,2,1,0:T(8,128)S(1)}, f32[3,2,2,64,256]{4,3,2,1,0:T(8,128)S(1)}, u32[]{:S(2)}, u32[]{:S(2)}) collective-permute-start(f32[3,2,2,64,256]{4,3,2,1,0:T(8,128)S(1)} %get-tuple-element.25), channel_id=1, source_target_pairs={{1,0},{2,1},{3,2},{4,3},{5,4},{6,5},{7,6},{8,7},{9,8},{10,9},{11,1... | collective-permute-start | bytes 2359304 | tf_op jit(solution)/shard_map/ppermute | solution.py:29
  197.9 17.5 %collective-permute-start.14 = (f32[3,2,2,64,256]{4,3,2,1,0:T(8,128)S(1)}, f32[3,2,2,64,256]{4,3,2,1,0:T(8,128)S(1)}, u32[]{:S(2)}, u32[]{:S(2)}) collective-permute-start(f32[3,2,2,64,256]{4,3,2,1,0:T(8,128)S(1)} %get-tuple-element.22), channel_id=1, source_target_pairs={{0,1},{1,2},{2,3},{3,4},{4,5},{5,6},{6,7},{7,8},{8,9},{9,10},{10,1... | collective-permute-start | bytes 2359304 | tf_op jit(solution)/shard_map/ppermute | solution.py:28
  213.5 6.1 %collective-permute-start.15 = (f32[3,2,2,64,256]{4,3,2,1,0:T(8,128)S(1)}, f32[3,2,2,64,256]{4,3,2,1,0:T(8,128)S(1)}, u32[]{:S(2)}, u32[]{:S(2)}) collective-permute-start(f32[3,2,2,64,256]{4,3,2,1,0:T(8,128)S(1)} %get-tuple-element.23), channel_id=1, source_target_pairs={{1,0},{2,1},{3,2},{4,3},{5,4},{6,5},{7,6},{8,7},{9,8},{10,9},{11,1... | collective-permute-start | bytes 2359304 | tf_op jit(solution)/shard_map/ppermute | solution.py:29
  223.3 4.7 %copy-start.4 = (f32[8,64,256]{2,1,0:T(8,128)S(1)}, f32[8,64,256]{2,1,0:T(8,128)}, u32[]{:S(2)}) copy-start(f32[8,64,256]{2,1,0:T(8,128)} %copy-done.3) | copy-start | bytes 1572868
  237.7 17.5 %collective-permute-start.16 = (f32[3,2,2,64,256]{4,3,2,1,0:T(8,128)S(1)}, f32[3,2,2,64,256]{4,3,2,1,0:T(8,128)S(1)}, u32[]{:S(2)}, u32[]{:S(2)}) collective-permute-start(f32[3,2,2,64,256]{4,3,2,1,0:T(8,128)S(1)} %get-tuple-element.20), channel_id=1, source_target_pairs={{0,1},{1,2},{2,3},{3,4},{4,5},{5,6},{6,7},{7,8},{8,9},{9,10},{10,1... | collective-permute-start | bytes 2359304 | tf_op jit(solution)/shard_map/ppermute | solution.py:28
  253.3 6.1 %collective-permute-start.17 = (f32[3,2,2,64,256]{4,3,2,1,0:T(8,128)S(1)}, f32[3,2,2,64,256]{4,3,2,1,0:T(8,128)S(1)}, u32[]{:S(2)}, u32[]{:S(2)}) collective-permute-start(f32[3,2,2,64,256]{4,3,2,1,0:T(8,128)S(1)} %get-tuple-element.21), channel_id=1, source_target_pairs={{1,0},{2,1},{3,2},{4,3},{5,4},{6,5},{7,6},{8,7},{9,8},{10,9},{11,1... | collective-permute-start | bytes 2359304 | tf_op jit(solution)/shard_map/ppermute | solution.py:29
  (2 other events, 1.6 us)

commit v2 on v0

v2 whole, which is shorter than its diff:
```python
import math

import jax
import jax.numpy as jnp
import ml_dtypes
import numpy as np
from jax import lax
from jax.experimental import pallas as pl
from jax.experimental.pallas import tpu as pltpu
from jax.sharding import PartitionSpec as P

RAD = 2
ROUNDS = 2
ITERS = 3

SIGMA = 1.5
STEP = 1.0
KAPPA = 0.5
EPS = 1e-05

LOCAL = 1
HS = max(1, RAD * LOCAL)
HT = HS + 1
HU = max(RAD, RAD * LOCAL)
HF = HU - RAD

MESH = pl.DeviceIdType.MESH


def taps_list(radius):
    raw = [math.exp(-(k * k) / (2.0 * SIGMA * SIGMA)) for k in range(-radius, radius + 1)]
    total = 0.0
    for value in raw:
        total = total + value
    return [value / total for value in raw]


def band(size):
    taps = taps_list(RAD)
    full = np.zeros((size, size), np.float64)
    for k in range(-RAD, RAD + 1):
        full += np.diag(np.full(size - abs(k), taps[k + RAD]), k)
    high = full.astype(np.float32).astype(ml_dtypes.bfloat16)
    low = (full - high.astype(np.float64)).astype(np.float32).astype(ml_dtypes.bfloat16)
    return high, low


def split(value):
    high = value.astype(jnp.bfloat16)
    low = (value - high.astype(jnp.float32)).astype(jnp.bfloat16)
    return high, low


def moved(value, axis, step):
    if step == 0:
        return value
    size = value.shape[axis]
    index = lax.broadcasted_iota(jnp.int32, value.shape, axis)
    edge = size - 1 if step > 0 else 0
    return jnp.where(index == edge, 0.0, pltpu.roll(value, (-step) % size, axis))


def kernel(n, subjects, template, wrow, wcol, atlas, fields_out,
           images, cur, grad, upd, fld, warped, mean, half_hi, half_lo, stats, tile,
           load_sem, in_send, in_recv, upd_send, upd_recv, mean_send, mean_recv,
           stat_send, stat_recv, out_sem):
    me = lax.axis_index("brick")
    count_s, planes, rows, cols = subjects.shape
    has_low, has_high = me > 0, me < n - 1
    first, last = me == 0, me == n - 1
    low, high = {"brick": me - 1}, {"brick": me + 1}
    total_planes = n * planes
    taps = taps_list(RAD)

    barrier = pltpu.get_barrier_semaphore()
    for k in range(1, n):
        pl.semaphore_signal(barrier, inc=1, device_id={"brick": lax.rem(me + k, n)}, device_id_type=MESH)
    pl.semaphore_wait(barrier, n - 1)

    def inside(p):
        place = me * planes + p
        return jnp.logical_and(place >= 0, place < total_planes)

    def faces(src, dst, halo, base_src, base_dst, lead, send, recv):
        up = pltpu.make_async_remote_copy(
            src_ref=src.at[lead + (pl.ds(base_src + planes - halo, halo),)],
            dst_ref=dst.at[lead + (pl.ds(base_dst - halo, halo),)],
            send_sem=send.at[0], recv_sem=recv.at[0], device_id=high, device_id_type=MESH)
        down = pltpu.make_async_remote_copy(
            src_ref=src.at[lead + (pl.ds(base_src, halo),)],
            dst_ref=dst.at[lead + (pl.ds(base_dst + planes, halo),)],
            send_sem=send.at[1], recv_sem=recv.at[1], device_id=low, device_id_type=MESH)
        return up, down

    def start(pair):
        pl.when(has_high)(lambda: pair[0].start())
        pl.when(has_low)(lambda: pair[1].start())

    def finish(pair):
        @pl.when(has_high)
        def _():
            pair[0].wait_send()
            pair[1].wait_recv()

        @pl.when(has_low)
        def _():
            pair[1].wait_send()
            pair[0].wait_recv()

    own = images.at[4]
    whole = slice(None)
    sub_pair = faces(subjects, own, HS, 0, HS, (whole,), in_send.at[0], in_recv.at[0])
    tem_pair = faces(template, cur, HT, 0, HT, (), in_send.at[1], in_recv.at[1])
    start(tem_pair)
    start(sub_pair)
    load_s = pltpu.make_async_copy(subjects, own.at[:, pl.ds(HS, planes)], load_sem.at[0])
    load_t = pltpu.make_async_copy(template, cur.at[pl.ds(HT, planes)], load_sem.at[1])
    load_s.start()
    load_t.start()

    def clear(ref, lead, halo, base):
        shape = (halo, rows, cols)

        @pl.when(first)
        def _():
            ref[lead + (pl.ds(base - halo, halo),)] = jnp.zeros(shape, jnp.float32)

        @pl.when(last)
        def _():
            ref[lead + (pl.ds(base + planes, halo),)] = jnp.zeros(shape, jnp.float32)

    clear(cur, (), HT, HT)
    for s in range(count_s):
        clear(images, (4, s), HS, HS)
        for slot in range(2):
            for k in range(3):
                clear(upd, (slot, s, k), HU, HU)

    def shift_planes(s, lo, hi):
        @pl.loop(lo + HS, hi + HS)
        def _(p):
            value = images[4, s, p]
            for c in (-1, 0, 1):
                side = moved(value, 1, c)
                for b in (-1, 0, 1):
                    if (b, c) != (0, 0):
                        images[(b + 1) * 3 + c + 1, s, p] = moved(side, 0, b)

    def gradients(lo, hi):
        @pl.loop(lo, hi)
        def _(p):
            here = cur[p + HT]
            g0 = (cur[p + HT + 1] - cur[p + HT - 1]) * 0.5
            g1 = (moved(here, 0, 1) - moved(here, 0, -1)) * 0.5
            g2 = (moved(here, 1, 1) - moved(here, 1, -1)) * 0.5
            grad[0, p + HU] = g0
            grad[1, p + HU] = g1
            grad[2, p + HU] = g2
            grad[3, p + HU] = g0 * g0 + g1 * g1 + g2 * g2 + KAPPA

    def chunks(lo, hi, body):
        per = rows // 8

        @pl.loop(0, (hi - lo) * per, unroll=2)
        def _(i):
            body(lo + i // per, pl.ds(pl.multiple_of((i % per) * 8, 8), 8))

    def warp(s, p, rs):
        u = [jnp.tanh(fld[s, k, p + HF, rs]) for k in range(3)]
        pos = [v > 0.0 for v in u]
        size = [jnp.abs(v) for v in u]

        def two(c):
            here, side = [], []
            for b in (0, 1, 2):
                where = b * 3 + c
                here.append(images[where, s, p + HS, rs])
                side.append(jnp.where(pos[0], images[where, s, p + HS + 1, rs], images[where, s, p + HS - 1, rs]))
            return (here[1], side[1], jnp.where(pos[1], here[2], here[0]), jnp.where(pos[1], side[2], side[0]))

        left, middle, right = two(0), two(1), two(2)
        beside = [jnp.where(pos[2], r, l) for r, l in zip(right, left)]
        lines = [m + size[2] * (o - m) for m, o in zip(middle, beside)]
        near = lines[0] + size[0] * (lines[1] - lines[0])
        far = lines[2] + size[0] * (lines[3] - lines[2])
        return near + size[1] * (far - near)

    def force(s, slot, lo, hi, kind):
        def body(p, rs):
            if kind == "subject":
                image = images[4, s, p + HS, rs]
            elif kind == "stored":
                image = warped[s, p, rs]
            else:
                image = warp(s, p, rs)
            diff = cur[p + HT, rs] - image
            ratio = STEP * diff / (grad[3, p + HU, rs] + diff * diff)
            for k in range(3):
                value = grad[k, p + HU, rs] * ratio
                if kind != "subject":
                    value = value + fld[s, k, p + HF, rs]
                if lo < 0:
                    value = jnp.where(inside(p), value, 0.0)
                upd[slot, s, k, p + HU, rs] = value

        chunks(lo, hi, body)

    def smooth(s, slot, lo, hi):
        number = hi - lo

        @pl.loop(0, 3)
        def _(k):
            @pl.loop(0, number)
            def _(i):
                at = i + lo + HU
                value = taps[2] * upd[slot, s, k, at]
                value = value + taps[1] * (upd[slot, s, k, at - 1] + upd[slot, s, k, at + 1])
                value = value + taps[0] * (upd[slot, s, k, at - 2] + upd[slot, s, k, at + 2])
                hi_part, lo_part = split(value)
                stack = jnp.concatenate([hi_part, lo_part, hi_part], axis=0)
                value = jnp.dot(wrow[...], stack, preferred_element_type=jnp.float32)
                hi_part, lo_part = split(value)
                half_hi[i] = hi_part
                half_lo[i] = lo_part

            a = half_hi[0:number].reshape(number * rows, cols)
            b = half_lo[0:number].reshape(number * rows, cols)
            stack = jnp.concatenate([a, b, a], axis=1)
            value = jnp.dot(stack, wcol[...], preferred_element_type=jnp.float32)
            fld[s, k, pl.ds(lo + HF, number)] = value.reshape(number, rows, cols)

    def exchange(s, slot):
        return faces(upd.at[slot, s], upd.at[slot, s], RAD, HU, HU, (whole,),
                     upd_send.at[slot, s], upd_recv.at[slot, s])

    def mean_image(keep):
        def body(p, rs):
            images_here = [warp(s, p, rs) for s in range(count_s)]
            if keep:
                for s in range(count_s):
                    warped[s, p, rs] = images_here[s]
            total = images_here[0]
            for value in images_here[1:]:
                total = total + value
            mean[p + 1, rs] = total * (1.0 / count_s)

        chunks(0, planes, body)

    def statistics(rnd, own_count):
        def add(p, total):
            return total + mean[p + 1]

        total = jnp.sum(lax.fori_loop(0, planes, add, jnp.zeros((rows, cols), jnp.float32)))
        center = total / own_count

        def square(p, total):
            away = mean[p + 1] - center
            return total + away * away

        spread = jnp.sum(lax.fori_loop(0, planes, square, jnp.zeros((rows, cols), jnp.float32)))
        lane = lax.broadcasted_iota(jnp.int32, (8, 128), 1)
        tile[rnd] = jnp.where(lane == 0, total, jnp.where(lane == 1, spread, 0.0))
        stats[rnd, 0] = tile[rnd]
        copies = []
        for k in range(1, n):
            copy = pltpu.make_async_remote_copy(
                src_ref=tile.at[rnd], dst_ref=stats.at[rnd, k],
                send_sem=stat_send.at[rnd, k], recv_sem=stat_recv.at[rnd, k],
                device_id={"brick": lax.rem(me + k, n)}, device_id_type=MESH)
            copy.start()
            copies.append(copy)
        for copy in copies:
            copy.wait()
        every = stats[rnd]
        lanes = lax.broadcasted_iota(jnp.int32, (n, 8, 128), 2)
        rows_of = lax.broadcasted_iota(jnp.int32, (n, 8, 128), 1)
        on_sum = jnp.logical_and(lanes == 0, rows_of == 0)
        on_spread = jnp.logical_and(lanes == 1, rows_of == 0)
        count = own_count * n
        mu = jnp.sum(jnp.where(on_sum, every, 0.0)) / count
        offsets = jnp.where(on_sum, every / own_count - mu, 0.0)
        var = (jnp.sum(jnp.where(on_spread, every, 0.0)) + own_count * jnp.sum(offsets * offsets)) / count
        scale = 1.0 / jnp.sqrt(jnp.full((8, cols), var + EPS, jnp.float32))
        return mu, scale

    own_count = float(planes * rows * cols)
    out_copies = []

    load_s.wait()
    for s in range(count_s):
        shift_planes(s, 0, planes)
    load_t.wait()
    finish(tem_pair)
    gradients(-HU if LOCAL else 0, planes + (HU if LOCAL else 0))
    finish(sub_pair)
    reach = HF + 1
    for s in range(count_s):
        shift_planes(s, -reach, 0)
        shift_planes(s, planes, planes + reach)

    pairs = {}
    for rnd in range(ROUNDS):
        for step in range(ITERS):
            slot = (rnd * ITERS + step) % 2
            local = rnd == 0 and step < LOCAL
            wide = RAD * (LOCAL - step) if local else 0
            kind = "warp" if step else ("stored" if rnd else "subject")
            for s in range(count_s):
                if step:
                    settle(s)
                force(s, slot, -wide, planes + wide, kind)
                if not local:
                    pairs[s] = exchange(s, slot)
                    start(pairs[s])

            def settle(s, slot=slot, local=local, wide=wide):
                if not local:
                    finish(pairs[s])
                grow = wide - RAD if local else 0
                smooth(s, slot, -grow, planes + grow)
        for s in range(count_s):
            settle(s)
            if rnd == ROUNDS - 1:
                for k in range(3):
                    copy = pltpu.make_async_copy(
                        fld.at[s, k, pl.ds(HF, planes)], fields_out.at[k, s], out_sem.at[s, k])
                    copy.start()
                    out_copies.append(copy)
        mean_image(rnd < ROUNDS - 1)
        more = rnd < ROUNDS - 1
        if more:
            pair = faces(mean, mean, 1, 1, 1, (), mean_send, mean_recv)
            start(pair)
        mu, scale = statistics(rnd, own_count)
        if more:
            finish(pair)
        reach_mean = 1 if more else 0

        def normal(p, rs):
            value = (mean[p + 1, rs] - mu) * scale
            if more:
                value = jnp.where(inside(p), value, 0.0)
            cur[p + HT, rs] = value

        if more:
            clear(mean, (), 1, 1)
        chunks(-reach_mean, planes + reach_mean, normal)
        if more:
            gradients(0, planes)
    copy = pltpu.make_async_copy(cur.at[pl.ds(HT, planes)], atlas, load_sem.at[1])
    copy.start()
    for other in out_copies:
        other.wait()
    copy.wait()


def per_device(subjects, template):
    n = lax.axis_size("brick")
    count_s, planes, rows, cols = subjects.shape
    row_hi, row_lo = band(rows)
    col_hi, col_lo = band(cols)
    wrow = jnp.asarray(np.concatenate([row_hi, row_hi, row_lo], axis=1))
    wcol = jnp.asarray(np.concatenate([col_hi, col_hi, col_lo], axis=0))
    anywhere = pl.BlockSpec(memory_space=pl.ANY)
    in_vmem = pl.BlockSpec(memory_space=pltpu.VMEM)
    dma = pltpu.SemaphoreType.DMA
    f32 = jnp.float32
    face = (rows, cols)
    atlas, fields = pl.pallas_call(
        lambda *refs: kernel(n, *refs),
        out_shape=(jax.ShapeDtypeStruct(template.shape, f32), jax.ShapeDtypeStruct((3,) + subjects.shape, f32)),
        in_specs=[anywhere, anywhere, in_vmem, in_vmem],
        out_specs=(anywhere, anywhere),
        scratch_shapes=[
            pltpu.VMEM((9, count_s, planes + 2 * HS) + face, f32),
            pltpu.VMEM((planes + 2 * HT,) + face, f32),
            pltpu.VMEM((4, planes + 2 * HU) + face, f32),
            pltpu.VMEM((2, count_s, 3, planes + 2 * HU) + face, f32),
            pltpu.VMEM((count_s, 3, planes + 2 * HF) + face, f32),
            pltpu.VMEM((count_s, planes) + face, f32),
            pltpu.VMEM((planes + 2,) + face, f32),
            pltpu.VMEM((planes + 2 * HF,) + face, jnp.bfloat16),
            pltpu.VMEM((planes + 2 * HF,) + face, jnp.bfloat16),
            pltpu.VMEM((ROUNDS, n, 8, 128), f32),
            pltpu.VMEM((ROUNDS, 8, 128), f32),
            dma((2,)),
            dma((2, 2)), dma((2, 2)),
            dma((2, count_s, 2)), dma((2, count_s, 2)),
            dma((2,)), dma((2,)),
            dma((ROUNDS, n)), dma((ROUNDS, n)),
            dma((count_s, 3)),
        ],
        compiler_params=pltpu.CompilerParams(
            collective_id=0, has_side_effects=True, vmem_limit_bytes=60 * 1024 * 1024),
    )(subjects, template, wrow, wcol)
    return atlas, fields


def solution(mesh):
    return jax.shard_map(
        per_device,
        mesh=mesh,
        in_specs=(P("group", "brick", None, None), P(("group", "brick"), None, None)),
        out_specs=(P(("group", "brick"), None, None), P(None, "group", "brick", None, None)),
        check_vma=False,
    )
```

time: 389 us -> 153 us (0.39); the launches traced: 384 us -> 153 us
  Pallas kernels: 0 us -> 147 us
  blocking collectives: 145 us -> 0 us
  other arithmetic: 111 us -> 0 us
  starting transfers between devices: 92.1 us -> 0 us
  waiting for transfers between devices: 26.3 us -> 0 us
    pallas_call x0 -> x1, Pallas kernels: none -> 147 us  [per_device(): pl.pallas_call(lambda *refs: kernel(n, *refs), out_shape=(jax.ShapeDtypeS...]
    psum x4 -> x0, blocking collectives: 145 us -> none  [the longest x2 84.2 us: normalize(): mu = lax.psum(jnp.sum(mean_image), 'brick') / count]
    ppermute x18 -> x0, starting transfers between devices: 92.1 us -> none  [the longest x9 78.7 us: padded_2(): before = lax.ppermute(last, axis, up)]
    div x8 -> x0, other arithmetic: 35.1 us -> none  [the longest x6 32.1 us: forces(): ratio = STEP * diff / denom]
    tanh x6 -> x0, other arithmetic: 28.3 us -> none  [per_device(): warped = warp_image(image_pad, jnp.tanh(fields))]
    ppermute x18 -> x0, waiting for transfers between devices: 26.3 us -> none  [the longest x9 23.9 us: padded_2(): after = lax.ppermute(initial, axis, down)]
    add x17 -> x0, other arithmetic: 25.6 us -> none  [the longest x6 11.5 us: first_pass(): result + taps[k] * lax.slice_in_dim(extended, k, k + planes, axis=2)]
    reduce_sum x6 -> x0, other arithmetic: 16.6 us -> none  [the longest x2 11.4 us: per_device(): current = normalize(jnp.mean(warped, axis=0), count)]
  transfers between devices with their start and end apart: 18 -> 0, of which waited for: 12 -> 0; matrix products, arithmetic and copies ran while one was open for 1% -> 0% of each run, Pallas kernels for 0% -> 0%
where the time goes in v2:
time: 153 us
  Pallas kernels  147 us (96%)
  local copies, waits for them, and re-layouts  5.78 us (4%)
    pallas_call x1, Pallas kernels, per_device(): pl.pallas_call(lambda *refs: kernel(n, *refs), out_shape=(jax.ShapeDtypeS...  147 us
    unnamed x2, local copies, waits for them, and re-layouts  5.78 us

profile of v2, /device:TPU:0, one launch (start us, length us, event | category | flops | bytes accessed | tf_op | source)
XLA Modules:
  0.0 153.1 jit_solution(11019332584398641951)
XLA Ops:
  0.6 146.7 %shard_map.59 = (f32[8,64,256]{2,1,0:T(8,128)}, f32[3,2,8,64,256]{4,3,2,1,0:T(8,128)}) custom-call(f32[2,8,64,256]{3,2,1,0:T(8,128)} %refs_0_.1, f32[8,64,256]{2,1,0:T(8,128)} %refs_1_.1, bf16[64,192]{1,0:T(8,128)(2,1)} %constant.4.clone.refs_2_, bf16[768,256]{1,0:T(8,128)(2,1)} %constant.5.clone.refs_3_), custom_call_target="tpu_custom_call" | custom-call | tf_op jit(solution)/shard_map/pallas_call | solution.py:369
  147.4 1.9 %copy.8 = f32[8,64,256]{2,1,0:T(8,128)} copy(f32[8,64,256]{2,1,0:T(8,128)} %get-tuple-element.4) | data formatting | bytes 1048576
  149.2 3.9 %copy.9 = f32[3,2,8,64,256]{4,3,2,1,0:T(8,128)} copy(f32[3,2,8,64,256]{4,3,2,1,0:T(8,128)} %get-tuple-element.5) | data formatting | bytes 6291456

commit v3 on v2

--- a/solution.py
+++ b/solution.py
@@ -210,7 +210,7 @@
 
         @pl.loop(0, 3)
         def _(k):
-            @pl.loop(0, number)
+            @pl.loop(0, number, unroll=number)
             def _(i):
                 at = i + lo + HU
                 value = taps[2] * upd[slot, s, k, at]

time: 153 us -> 145 us (0.948)
  Pallas kernels: 147 us -> 139 us
    pallas_call x1, Pallas kernels: 147 us -> 139 us  [per_device(): pl.pallas_call(lambda *refs: kernel(n, *refs), out_shape=(jax.ShapeDtypeS...]
where the time goes in v3:
time: 145 us
  Pallas kernels  139 us (96%)
  local copies, waits for them, and re-layouts  5.78 us (4%)
    pallas_call x1, Pallas kernels, per_device(): pl.pallas_call(lambda *refs: kernel(n, *refs), out_shape=(jax.ShapeDtypeS...  139 us
    unnamed x2, local copies, waits for them, and re-layouts  5.78 us

profile of v3, /device:TPU:0, one launch (start us, length us, event | category | flops | bytes accessed | tf_op | source)
XLA Modules:
  0.0 145.2 jit_solution(7814545680763474524)
XLA Ops:
  0.6 138.8 %shard_map.59 = (f32[8,64,256]{2,1,0:T(8,128)}, f32[3,2,8,64,256]{4,3,2,1,0:T(8,128)}) custom-call(f32[2,8,64,256]{3,2,1,0:T(8,128)} %refs_0_.1, f32[8,64,256]{2,1,0:T(8,128)} %refs_1_.1, bf16[64,192]{1,0:T(8,128)(2,1)} %constant.4.clone.refs_2_, bf16[768,256]{1,0:T(8,128)(2,1)} %constant.5.clone.refs_3_), custom_call_target="tpu_custom_call" | custom-call | tf_op jit(solution)/shard_map/pallas_call | solution.py:369
  139.4 1.9 %copy.8 = f32[8,64,256]{2,1,0:T(8,128)} copy(f32[8,64,256]{2,1,0:T(8,128)} %get-tuple-element.4) | data formatting | bytes 1048576
  141.3 3.9 %copy.9 = f32[3,2,8,64,256]{4,3,2,1,0:T(8,128)} copy(f32[3,2,8,64,256]{4,3,2,1,0:T(8,128)} %get-tuple-element.5) | data formatting | bytes 6291456

commit v4 on v3

--- a/solution.py
+++ b/solution.py
@@ -18,7 +18,7 @@
 KAPPA = 0.5
 EPS = 1e-05
 
-LOCAL = 1
+LOCAL = 2
 HS = max(1, RAD * LOCAL)
 HT = HS + 1
 HU = max(RAD, RAD * LOCAL)
@@ -109,10 +109,12 @@
 
     own = images.at[4]
     whole = slice(None)
-    sub_pair = faces(subjects, own, HS, 0, HS, (whole,), in_send.at[0], in_recv.at[0])
-    tem_pair = faces(template, cur, HT, 0, HT, (), in_send.at[1], in_recv.at[1])
+    sub_pairs = [faces(subjects, own, HS, 0, HS, (s,), in_send.at[1 + s], in_recv.at[1 + s])
+                 for s in range(count_s)]
+    tem_pair = faces(template, cur, HT, 0, HT, (), in_send.at[0], in_recv.at[0])
     start(tem_pair)
-    start(sub_pair)
+    for pair in sub_pairs:
+        start(pair)
     load_s = pltpu.make_async_copy(subjects, own.at[:, pl.ds(HS, planes)], load_sem.at[0])
     load_t = pltpu.make_async_copy(template, cur.at[pl.ds(HT, planes)], load_sem.at[1])
     load_s.start()
@@ -161,7 +163,7 @@
     def chunks(lo, hi, body):
         per = rows // 8
 
-        @pl.loop(0, (hi - lo) * per, unroll=2)
+        @pl.loop(0, (hi - lo) * per, unroll=4)
         def _(i):
             body(lo + i // per, pl.ds(pl.multiple_of((i % per) * 8, 8), 8))
 
@@ -292,34 +294,37 @@
     load_t.wait()
     finish(tem_pair)
     gradients(-HU if LOCAL else 0, planes + (HU if LOCAL else 0))
-    finish(sub_pair)
     reach = HF + 1
-    for s in range(count_s):
-        shift_planes(s, -reach, 0)
-        shift_planes(s, planes, planes + reach)
-
     pairs = {}
+
+    def advance(rnd, step, s):
+        slot = (rnd * ITERS + step) % 2
+        force(s, slot, 0, planes, "warp" if step else ("stored" if rnd else "subject"))
+        pairs[s] = exchange(s, slot)
+        start(pairs[s])
+
     for rnd in range(ROUNDS):
-        for step in range(ITERS):
-            slot = (rnd * ITERS + step) % 2
-            local = rnd == 0 and step < LOCAL
-            wide = RAD * (LOCAL - step) if local else 0
-            kind = "warp" if step else ("stored" if rnd else "subject")
+        head = LOCAL if rnd == 0 else 0
+        for s in range(count_s):
+            if rnd == 0:
+                finish(sub_pairs[s])
+                shift_planes(s, -reach, 0)
+                shift_planes(s, planes, planes + reach)
+            for step in range(head):
+                wide = RAD * (LOCAL - step)
+                force(s, (LOCAL + 1) % 2, -wide, planes + wide, "warp" if step else "subject")
+                smooth(s, (LOCAL + 1) % 2, RAD - wide, planes + wide - RAD)
+            if head < ITERS:
+                advance(rnd, head, s)
+        for step in range(head + 1, ITERS):
             for s in range(count_s):
-                if step:
-                    settle(s)
-                force(s, slot, -wide, planes + wide, kind)
-                if not local:
-                    pairs[s] = exchange(s, slot)
-                    start(pairs[s])
-
-            def settle(s, slot=slot, local=local, wide=wide):
-                if not local:
-                    finish(pairs[s])
-                grow = wide - RAD if local else 0
-                smooth(s, slot, -grow, planes + grow)
+                finish(pairs[s])
+                smooth(s, (rnd * ITERS + step - 1) % 2, 0, planes)
+                advance(rnd, step, s)
         for s in range(count_s):
-            settle(s)
+            if head < ITERS:
+                finish(pairs[s])
+                smooth(s, (rnd * ITERS + ITERS - 1) % 2, 0, planes)
             if rnd == ROUNDS - 1:
                 for k in range(3):
                     copy = pltpu.make_async_copy(
@@ -384,7 +389,7 @@
             pltpu.VMEM((ROUNDS, n, 8, 128), f32),
             pltpu.VMEM((ROUNDS, 8, 128), f32),
             dma((2,)),
-            dma((2, 2)), dma((2, 2)),
+            dma((1 + count_s, 2)), dma((1 + count_s, 2)),
             dma((2, count_s, 2)), dma((2, count_s, 2)),
             dma((2,)), dma((2,)),
             dma((ROUNDS, n)), dma((ROUNDS, n)),

time: 145 us -> 137 us (0.945)
  Pallas kernels: 139 us -> 131 us
    pallas_call x1, Pallas kernels: 139 us -> 131 us  [per_device(): pl.pallas_call(lambda *refs: kernel(n, *refs), out_shape=(jax.ShapeDtypeS...]
where the time goes in v4:
time: 137 us
  Pallas kernels  131 us (96%)
  local copies, waits for them, and re-layouts  5.78 us (4%)
    pallas_call x1, Pallas kernels, per_device(): pl.pallas_call(lambda *refs: kernel(n, *refs), out_shape=(jax.ShapeDtypeS...  131 us
    unnamed x2, local copies, waits for them, and re-layouts  5.78 us

profile of v4, /device:TPU:0, one launch (start us, length us, event | category | flops | bytes accessed | tf_op | source)
XLA Modules:
  0.0 137.0 jit_solution(9579927691933625775)
XLA Ops:
  0.6 130.6 %shard_map.59 = (f32[8,64,256]{2,1,0:T(8,128)}, f32[3,2,8,64,256]{4,3,2,1,0:T(8,128)}) custom-call(f32[2,8,64,256]{3,2,1,0:T(8,128)} %refs_0_.1, f32[8,64,256]{2,1,0:T(8,128)} %refs_1_.1, bf16[64,192]{1,0:T(8,128)(2,1)} %constant.4.clone.refs_2_, bf16[768,256]{1,0:T(8,128)(2,1)} %constant.5.clone.refs_3_), custom_call_target="tpu_custom_call" | custom-call | tf_op jit(solution)/shard_map/pallas_call | solution.py:374
  131.3 1.9 %copy.8 = f32[8,64,256]{2,1,0:T(8,128)} copy(f32[8,64,256]{2,1,0:T(8,128)} %get-tuple-element.4) | data formatting | bytes 1048576
  133.1 3.9 %copy.9 = f32[3,2,8,64,256]{4,3,2,1,0:T(8,128)} copy(f32[3,2,8,64,256]{4,3,2,1,0:T(8,128)} %get-tuple-element.5) | data formatting | bytes 6291456

commit v5 on v4

--- a/solution.py
+++ b/solution.py
@@ -299,9 +299,12 @@
 
     def advance(rnd, step, s):
         slot = (rnd * ITERS + step) % 2
-        force(s, slot, 0, planes, "warp" if step else ("stored" if rnd else "subject"))
+        kind = "warp" if step else ("stored" if rnd else "subject")
+        force(s, slot, 0, RAD, kind)
+        force(s, slot, planes - RAD, planes, kind)
         pairs[s] = exchange(s, slot)
         start(pairs[s])
+        force(s, slot, RAD, planes - RAD, kind)
 
     for rnd in range(ROUNDS):
         head = LOCAL if rnd == 0 else 0

time: 137 us -> 135 us (0.985)
  Pallas kernels: 131 us -> 128 us
    pallas_call x1, Pallas kernels: 131 us -> 128 us  [per_device(): pl.pallas_call(lambda *refs: kernel(n, *refs), out_shape=(jax.ShapeDtypeS...]
where the time goes in v5:
time: 135 us; the launch traced here: 134 us
  Pallas kernels  128 us (95%)
  local copies, waits for them, and re-layouts  5.78 us (4%)
    pallas_call x1, Pallas kernels, per_device(): pl.pallas_call(lambda *refs: kernel(n, *refs), out_shape=(jax.ShapeDtypeS...  128 us
    unnamed x2, local copies, waits for them, and re-layouts  5.78 us

profile of v5, /device:TPU:0, one launch (start us, length us, event | category | flops | bytes accessed | tf_op | source)
XLA Modules:
  0.0 134.4 jit_solution(11186083902728995291)
XLA Ops:
  0.6 128.0 %shard_map.59 = (f32[8,64,256]{2,1,0:T(8,128)}, f32[3,2,8,64,256]{4,3,2,1,0:T(8,128)}) custom-call(f32[2,8,64,256]{3,2,1,0:T(8,128)} %refs_0_.1, f32[8,64,256]{2,1,0:T(8,128)} %refs_1_.1, bf16[64,192]{1,0:T(8,128)(2,1)} %constant.4.clone.refs_2_, bf16[768,256]{1,0:T(8,128)(2,1)} %constant.5.clone.refs_3_), custom_call_target="tpu_custom_call" | custom-call | tf_op jit(solution)/shard_map/pallas_call | solution.py:377
  128.7 1.9 %copy.8 = f32[8,64,256]{2,1,0:T(8,128)} copy(f32[8,64,256]{2,1,0:T(8,128)} %get-tuple-element.4) | data formatting | bytes 1048576
  130.5 3.9 %copy.9 = f32[3,2,8,64,256]{4,3,2,1,0:T(8,128)} copy(f32[3,2,8,64,256]{4,3,2,1,0:T(8,128)} %get-tuple-element.5) | data formatting | bytes 6291456
